TPU v7x, 32 devices: a whole 2x2x4 slice. The times are simulated.
32 devices in a mesh: seq: 16 (over z, y, x), frm: 2 (over core).
Axes of the slice: x: 2, y: 2, z: 4, core: 2. Of those that a mesh axis runs over, the one named last changes fastest.
Arguments:
- hidden: bfloat16 [32, 448, 768], P('seq'), may hold values from -6 to 6
- encoder: bfloat16 [32, 1500, 768], P('seq', 'frm'), may hold values from -6 to 6
- cotangent: bfloat16 [32, 448, 768], P('seq'), may hold values from -6 to 6
- lengths: int32 [32], P('seq'), may hold values from 56 to 448
- frame_counts: int32 [32], P('seq'), may hold values from 187 to 1500
- corpus_ids: int32 [32], P('seq'), may hold values from 0 to 8
- corpus_weights: float32 [9], replicated, may hold values from 0.25 to 4
- first_gain: float32 [768], replicated, may hold values from 0.5 to 1.5
- first_shift: float32 [768], replicated, may hold values from -1.25 to 1.25
- self_query: bfloat16 [768, 768], replicated, may hold values from -0.21875 to 0.21875
- self_query_bias: float32 [768], replicated, may hold values from -3 to 3
- self_key: bfloat16 [768, 768], replicated, may hold values from -0.21875 to 0.21875
- self_value: bfloat16 [768, 768], replicated, may hold values from -0.21875 to 0.21875
- self_value_bias: float32 [768], replicated, may hold values from -3 to 3
- self_out: bfloat16 [768, 768], replicated, may hold values from -1.75 to 1.75
- self_out_bias: float32 [768], replicated, may hold values from -1.75 to 1.75
- second_gain: float32 [768], replicated, may hold values from 0.5 to 1.5
- second_shift: float32 [768], replicated, may hold values from -1.25 to 1.25
- cross_query: bfloat16 [768, 768], replicated, may hold values from -0.21875 to 0.21875
- cross_query_bias: float32 [768], replicated, may hold values from -3 to 3
- cross_key: bfloat16 [768, 768], replicated, may hold values from -0.21875 to 0.21875
- cross_value: bfloat16 [768, 768], replicated, may hold values from -0.21875 to 0.21875
- cross_value_bias: float32 [768], replicated, may hold values from -3 to 3
- cross_out: bfloat16 [768, 768], replicated, may hold values from -2.5 to 2.5
- cross_out_bias: float32 [768], replicated, may hold values from -1.75 to 1.75
- third_gain: float32 [768], replicated, may hold values from 0.5 to 1.5
- third_shift: float32 [768], replicated, may hold values from -1.25 to 1.25
- expand_weight: bfloat16 [768, 3072], replicated, may hold values from -0.21875 to 0.21875
- expand_bias: float32 [3072], replicated, may hold values from -3 to 3
- shrink_weight: bfloat16 [3072, 768], replicated, may hold values from -0.109375 to 0.109375
- shrink_bias: float32 [768], replicated, may hold values from -1.75 to 1.75
Outputs:
- output: bfloat16 [32, 448, 768], P('seq')
- grad_hidden: float32 [32, 448, 768], P('seq')
- grad_encoder: float32 [32, 1500, 768], P('seq', 'frm')
- grad_first_gain: float32 [768], P('seq')
- grad_first_shift: float32 [768], P('seq')
- grad_self_query: float32 [768, 768], P(None, 'seq')
- grad_self_query_bias: float32 [768], P('seq')
- grad_self_key: float32 [768, 768], P(None, 'seq')
- grad_self_value: float32 [768, 768], P(None, 'seq')
- grad_self_value_bias: float32 [768], P('seq')
- grad_self_out: float32 [768, 768], P(None, 'seq')
- grad_self_out_bias: float32 [768], P('seq')
- grad_second_gain: float32 [768], P('seq')
- grad_second_shift: float32 [768], P('seq')
- grad_cross_query: float32 [768, 768], P(None, 'seq')
- grad_cross_query_bias: float32 [768], P('seq')
- grad_cross_key: float32 [768, 768], P(None, 'seq')
- grad_cross_value: float32 [768, 768], P(None, 'seq')
- grad_cross_value_bias: float32 [768], P('seq')
- grad_cross_out: float32 [768, 768], P(None, 'seq')
- grad_cross_out_bias: float32 [768], P('seq')
- grad_third_gain: float32 [768], P('seq')
- grad_third_shift: float32 [768], P('seq')
- grad_expand_weight: float32 [768, 3072], P(None, 'seq')
- grad_expand_bias: float32 [3072], P('seq')
- grad_shrink_weight: float32 [3072, 768], P(None, 'seq')
- grad_shrink_bias: float32 [768], P('seq')
All inputs are finite; a program needn't handle non-finite values.
Results may differ from a plain program's by a relative error of at most 0.022.
Values may be sent and summed in bfloat16 or wider, within the bound.
A program may use at most 384 MiB of HBM per device.

v0:
```python
import jax
import jax.numpy as jnp
from jax import lax
from jax.sharding import PartitionSpec as P

HEADS = 12
HDIM = 64


def for_sending(shard):
    return jax.tree.map(lambda a: a.astype(jnp.bfloat16) if a.dtype == jnp.float32 else a, shard)


def matmul(left, right):
    return jnp.dot(left, right, preferred_element_type=jnp.float32)


def matmul_right_t(left, right):
    return lax.dot_general(
        left, right, (((1,), (1,)), ((), ())), preferred_element_type=jnp.float32
    )


def matmul_left_t(left, right):
    return lax.dot_general(
        left, right, (((0,), (0,)), ((), ())), preferred_element_type=jnp.float32
    )


def normalize(value, gain, shift):
    center = jnp.mean(value, axis=-1, keepdims=True)
    centered = value - center
    rstd = lax.rsqrt(jnp.mean(centered * centered, axis=-1, keepdims=True) + 1e-05)
    unit = centered * rstd
    return (unit * gain + shift, unit, rstd)


def normalize_back(grad, unit, rstd, gain):
    scaled = grad * gain
    return rstd * (
        scaled
        - jnp.mean(scaled, axis=-1, keepdims=True)
        - unit * jnp.mean(scaled * unit, axis=-1, keepdims=True)
    )


def heads_view(value, num_trans):
    return value.reshape(num_trans, value.shape[0] // num_trans, HEADS, HDIM)


def attention_scores(queries, key_rows, key_mask):
    scores = jnp.einsum("tqhd,tkhd->thqk", queries, key_rows, preferred_element_type=jnp.float32)
    return jnp.where(key_mask, scores, -1e30)


def local_softmax(scores):
    row_top = jnp.max(scores, axis=-1, keepdims=True)
    weights = jnp.exp(scores - row_top)
    return weights / jnp.sum(weights, axis=-1, keepdims=True)


def weigh_values(probs_low, value_rows):
    return jnp.einsum("thqk,tkhd->tqhd", probs_low, value_rows, preferred_element_type=jnp.float32)


def score_grads(dmix, value_rows):
    return jnp.einsum("tqhd,tkhd->thqk", dmix, value_rows, preferred_element_type=jnp.float32)


def attention_back(probs, probs_low, dprob, inner, queries, key_rows, dmix):
    dscore = (probs * (dprob - inner)).astype(jnp.bfloat16)
    dquery = jnp.einsum("thqk,tkhd->tqhd", dscore, key_rows, preferred_element_type=jnp.float32)
    dkeys = jnp.einsum("thqk,tqhd->tkhd", dscore, queries, preferred_element_type=jnp.float32)
    dvalues = jnp.einsum("thqk,tqhd->tkhd", probs_low, dmix, preferred_element_type=jnp.float32)
    return (dquery, dkeys, dvalues)


def exact_gelu(value):
    return jax.nn.gelu(value, approximate=False)


def shards(
    hidden,
    encoder,
    cotangent,
    lengths,
    frame_counts,
    corpus_ids,
    corpus_weights,
    first_gain,
    first_shift,
    self_query,
    self_query_bias,
    self_key,
    self_value,
    self_value_bias,
    self_out,
    self_out_bias,
    second_gain,
    second_shift,
    cross_query,
    cross_query_bias,
    cross_key,
    cross_value,
    cross_value_bias,
    cross_out,
    cross_out_bias,
    third_gain,
    third_shift,
    expand_weight,
    expand_bias,
    shrink_weight,
    shrink_bias,
):
    num_trans, num_slots, width = hidden.shape
    local_frames = encoder.shape[1]
    total_rows = num_trans * num_slots
    scale = HDIM ** (-0.5)
    scale_low = jnp.asarray(scale, jnp.bfloat16)
    frame_rank = lax.axis_index("frm")
    share = total_rows // lax.axis_size("frm")
    share_start = frame_rank * share

    def my_rows(value):
        return lax.dynamic_slice_in_dim(value, share_start, share, 0)

    def weight_grad(left, right):
        return matmul_left_t(my_rows(left), my_rows(right))

    def vector_grad(value):
        return jnp.sum(my_rows(value).astype(jnp.float32), axis=0)

    slot_index = jnp.arange(num_slots)
    self_mask = (
        (slot_index[:, None] >= slot_index[None, :])[None]
        & (slot_index[None, None, :] < lengths[:, None, None])
    )[:, None]
    inputs = hidden.reshape(total_rows, width).astype(jnp.float32)
    normed_one, unit_one, rstd_one = normalize(inputs, first_gain, first_shift)
    low_one = normed_one.astype(jnp.bfloat16)
    queries = ((matmul(low_one, self_query) + self_query_bias) * scale).astype(jnp.bfloat16)
    key_rows = matmul(low_one, self_key).astype(jnp.bfloat16)
    value_rows = (matmul(low_one, self_value) + self_value_bias).astype(jnp.bfloat16)
    query_heads = heads_view(queries, num_trans)
    key_heads = heads_view(key_rows, num_trans)
    value_heads = heads_view(value_rows, num_trans)
    probs = local_softmax(attention_scores(query_heads, key_heads, self_mask))
    probs_low = probs.astype(jnp.bfloat16)
    mixture = weigh_values(probs_low, value_heads).reshape(total_rows, width).astype(jnp.bfloat16)
    after_self = inputs + matmul(mixture, self_out) + self_out_bias
    normed_two, unit_two, rstd_two = normalize(after_self, second_gain, second_shift)
    low_two = normed_two.astype(jnp.bfloat16)
    cross_queries = ((matmul(low_two, cross_query) + cross_query_bias) * scale).astype(jnp.bfloat16)
    cross_query_heads = heads_view(cross_queries, num_trans)
    frame_first = frame_rank * local_frames
    frame_count = encoder.shape[1]
    state_rows = encoder.reshape(num_trans * frame_count, width)
    cross_keys = matmul(state_rows, cross_key).astype(jnp.bfloat16)
    cross_values = (matmul(state_rows, cross_value) + cross_value_bias).astype(jnp.bfloat16)
    cross_key_heads = heads_view(cross_keys, num_trans)
    cross_value_heads = heads_view(cross_values, num_trans)
    frame_index = frame_first + jnp.arange(frame_count)
    cross_mask = (frame_index[None, :] < frame_counts[:, None])[:, None, None, :]
    cross_scores = attention_scores(cross_query_heads, cross_key_heads, cross_mask)
    local_top = jnp.max(cross_scores, axis=-1, keepdims=True)
    row_top = lax.pmax(local_top.astype(jnp.bfloat16), "frm").astype(local_top.dtype)
    weights = jnp.exp(cross_scores - row_top)
    row_total = lax.psum(
        jnp.sum(weights, axis=-1, keepdims=True).astype(jnp.bfloat16), "frm"
    ).astype(jnp.float32)
    cross_probs = weights / row_total
    cross_probs_low = cross_probs.astype(jnp.bfloat16)
    cross_sum = lax.psum(
        weigh_values(cross_probs_low, cross_value_heads).astype(jnp.bfloat16), "frm"
    ).astype(jnp.float32)
    cross_mixture = cross_sum.reshape(total_rows, width).astype(jnp.bfloat16)
    after_cross = after_self + matmul(cross_mixture, cross_out) + cross_out_bias
    normed_three, unit_three, rstd_three = normalize(after_cross, third_gain, third_shift)
    low_three = normed_three.astype(jnp.bfloat16)
    pre_active = matmul(low_three, expand_weight) + expand_bias
    active, gelu_back = jax.vjp(exact_gelu, pre_active)
    active_low = active.astype(jnp.bfloat16)
    result = after_cross + matmul(active_low, shrink_weight) + shrink_bias
    output = result.astype(jnp.bfloat16).reshape(num_trans, num_slots, width)
    corpus_hit = (corpus_ids[:, None] == jnp.arange(corpus_weights.shape[0])[None, :]).astype(
        jnp.float32
    )
    row_scale = jnp.sum(corpus_hit * corpus_weights[None, :], axis=1)
    live_rows = (slot_index[None, :] < lengths[:, None]).astype(jnp.float32) * row_scale[:, None]
    grad_result = (cotangent.astype(jnp.float32) * live_rows[:, :, None]).reshape(total_rows, width)
    dshrink = grad_result.astype(jnp.bfloat16)
    grad_shrink_weight = weight_grad(active_low, dshrink)
    grad_shrink_bias = vector_grad(dshrink)
    dactive = matmul_right_t(dshrink, shrink_weight).astype(jnp.bfloat16)
    dpre = gelu_back(dactive.astype(jnp.float32))[0].astype(jnp.bfloat16)
    grad_expand_weight = weight_grad(low_three, dpre)
    grad_expand_bias = vector_grad(dpre)
    dnormed_three = matmul_right_t(dpre, expand_weight)
    grad_third_gain = jnp.sum(my_rows(dnormed_three * unit_three), axis=0)
    grad_third_shift = jnp.sum(my_rows(dnormed_three), axis=0)
    dafter_cross = grad_result + normalize_back(dnormed_three, unit_three, rstd_three, third_gain)
    dcross = dafter_cross.astype(jnp.bfloat16)
    grad_cross_out = weight_grad(cross_mixture, dcross)
    grad_cross_out_bias = vector_grad(dcross)
    dcross_mix = heads_view(matmul_right_t(dcross, cross_out).astype(jnp.bfloat16), num_trans)
    dcross_prob = score_grads(dcross_mix, cross_value_heads)
    inner_part = jnp.sum(cross_probs * dcross_prob, axis=-1, keepdims=True)
    cross_inner = lax.psum(inner_part.astype(jnp.bfloat16), "frm").astype(jnp.float32)
    dcq_part, dck_all, dcv_all = attention_back(
        cross_probs,
        cross_probs_low,
        dcross_prob,
        cross_inner,
        cross_query_heads,
        cross_key_heads,
        dcross_mix,
    )
    dcq_total = lax.psum(dcq_part.astype(jnp.bfloat16), "frm").astype(jnp.float32)
    dcq_scaled = dcq_total.reshape(total_rows, width).astype(jnp.bfloat16) * scale_low
    grad_cross_query = weight_grad(low_two, dcq_scaled)
    grad_cross_query_bias = vector_grad(dcq_scaled)
    dnormed_two = matmul_right_t(dcq_scaled, cross_query)
    local_states = encoder.reshape(num_trans * local_frames, width)
    dck_rows = dck_all.reshape(num_trans * local_frames, width).astype(jnp.bfloat16)
    dcv_rows = dcv_all.reshape(num_trans * local_frames, width).astype(jnp.bfloat16)
    grad_cross_key = matmul_left_t(local_states, dck_rows)
    grad_cross_value = matmul_left_t(local_states, dcv_rows)
    grad_cross_value_bias = jnp.sum(dcv_rows.astype(jnp.float32), axis=0)
    grad_encoder = (
        matmul_right_t(dck_rows, cross_key) + matmul_right_t(dcv_rows, cross_value)
    ).reshape(num_trans, local_frames, width)
    grad_second_gain = jnp.sum(my_rows(dnormed_two * unit_two), axis=0)
    grad_second_shift = jnp.sum(my_rows(dnormed_two), axis=0)
    dafter_self = dafter_cross + normalize_back(dnormed_two, unit_two, rstd_two, second_gain)
    dself = dafter_self.astype(jnp.bfloat16)
    grad_self_out = weight_grad(mixture, dself)
    grad_self_out_bias = vector_grad(dself)
    dself_mix = heads_view(matmul_right_t(dself, self_out).astype(jnp.bfloat16), num_trans)
    dself_prob = score_grads(dself_mix, value_heads)
    self_inner = jnp.sum(probs * dself_prob, axis=-1, keepdims=True)
    dquery, dkeys, dvalues = attention_back(
        probs, probs_low, dself_prob, self_inner, query_heads, key_heads, dself_mix
    )
    dquery_scaled = dquery.reshape(total_rows, width).astype(jnp.bfloat16) * scale_low
    dkey_rows = dkeys.reshape(total_rows, width).astype(jnp.bfloat16)
    dvalue_rows = dvalues.reshape(total_rows, width).astype(jnp.bfloat16)
    grad_self_query = weight_grad(low_one, dquery_scaled)
    grad_self_query_bias = vector_grad(dquery_scaled)
    grad_self_key = weight_grad(low_one, dkey_rows)
    grad_self_value = weight_grad(low_one, dvalue_rows)
    grad_self_value_bias = vector_grad(dvalue_rows)
    dnormed_one = (
        matmul_right_t(dquery_scaled, self_query)
        + matmul_right_t(dkey_rows, self_key)
        + matmul_right_t(dvalue_rows, self_value)
    )
    grad_first_gain = jnp.sum(my_rows(dnormed_one * unit_one), axis=0)
    grad_first_shift = jnp.sum(my_rows(dnormed_one), axis=0)
    grad_inputs = dafter_self + normalize_back(dnormed_one, unit_one, rstd_one, first_gain)
    parts = (
        lax.psum_scatter(grad_first_gain, "seq", scatter_dimension=0, tiled=True),
        lax.psum_scatter(grad_first_shift, "seq", scatter_dimension=0, tiled=True),
        lax.psum_scatter(grad_self_query, "seq", scatter_dimension=1, tiled=True),
        lax.psum_scatter(grad_self_query_bias, "seq", scatter_dimension=0, tiled=True),
        lax.psum_scatter(grad_self_key, "seq", scatter_dimension=1, tiled=True),
        lax.psum_scatter(grad_self_value, "seq", scatter_dimension=1, tiled=True),
        lax.psum_scatter(grad_self_value_bias, "seq", scatter_dimension=0, tiled=True),
        lax.psum_scatter(grad_self_out, "seq", scatter_dimension=1, tiled=True),
        lax.psum_scatter(grad_self_out_bias, "seq", scatter_dimension=0, tiled=True),
        lax.psum_scatter(grad_second_gain, "seq", scatter_dimension=0, tiled=True),
        lax.psum_scatter(grad_second_shift, "seq", scatter_dimension=0, tiled=True),
        lax.psum_scatter(grad_cross_query, "seq", scatter_dimension=1, tiled=True),
        lax.psum_scatter(grad_cross_query_bias, "seq", scatter_dimension=0, tiled=True),
        lax.psum_scatter(grad_cross_key, "seq", scatter_dimension=1, tiled=True),
        lax.psum_scatter(grad_cross_value, "seq", scatter_dimension=1, tiled=True),
        lax.psum_scatter(grad_cross_value_bias, "seq", scatter_dimension=0, tiled=True),
        lax.psum_scatter(grad_cross_out, "seq", scatter_dimension=1, tiled=True),
        lax.psum_scatter(grad_cross_out_bias, "seq", scatter_dimension=0, tiled=True),
        lax.psum_scatter(grad_third_gain, "seq", scatter_dimension=0, tiled=True),
        lax.psum_scatter(grad_third_shift, "seq", scatter_dimension=0, tiled=True),
        lax.psum_scatter(grad_expand_weight, "seq", scatter_dimension=1, tiled=True),
        lax.psum_scatter(grad_expand_bias, "seq", scatter_dimension=0, tiled=True),
        lax.psum_scatter(grad_shrink_weight, "seq", scatter_dimension=1, tiled=True),
        lax.psum_scatter(grad_shrink_bias, "seq", scatter_dimension=0, tiled=True),
    )
    summed = tuple(
        jax.tree.map(
            lambda part: part.astype(jnp.float32), lax.psum(for_sending(tuple(parts)), "frm")
        )
    )
    return (output, grad_inputs.reshape(num_trans, num_slots, width), grad_encoder) + tuple(summed)


def solution(mesh):
    return jax.shard_map(
        shards,
        mesh=mesh,
        in_specs=(
            P("seq", None, None),
            P("seq", "frm", None),
            P("seq", None, None),
            P("seq"),
            P("seq"),
            P("seq"),
            P(),
            P(),
            P(),
            P(),
            P(),
            P(),
            P(),
            P(),
            P(),
            P(),
            P(),
            P(),
            P(),
            P(),
            P(),
            P(),
            P(),
            P(),
            P(),
            P(),
            P(),
            P(),
            P(),
            P(),
            P(),
        ),
        out_specs=(
            P("seq", None, None),
            P("seq", None, None),
            P("seq", "frm", None),
            P("seq"),
            P("seq"),
            P(None, "seq"),
            P("seq"),
            P(None, "seq"),
            P(None, "seq"),
            P("seq"),
            P(None, "seq"),
            P("seq"),
            P("seq"),
            P("seq"),
            P(None, "seq"),
            P("seq"),
            P(None, "seq"),
            P(None, "seq"),
            P("seq"),
            P(None, "seq"),
            P("seq"),
            P("seq"),
            P("seq"),
            P(None, "seq"),
            P("seq"),
            P(None, "seq"),
            P("seq"),
        ),
        check_vma=False,
    )
```

profile of v0, /device:TPU:0, one launch (start us, length us, event | category | flops | bytes accessed | tf_op | source)
XLA Modules:
  0.0 1912.7 jit_solution(10211657822465803796)
XLA Ops:
  78.8 13.4 fusion.137
  127.3 14.9 select_reduce_fusion
  147.2 15.0 fusion.2
  168.0 13.4 fusion.71
  188.9 19.1 all-reduce.21.cloned.1.call-done
  214.9 31.3 %multiply_convert_fusion.2 = (bf16[896,3072]{1,0:T(8,128)(2,1)}, f32[896,3072]{1,0:T(8,128)}, f32[896,3072]{1,0:T(8,128)}) fusion(f32[3072]{0:T(1024)S(1)} %copy-done.85, bf16[896,768]{1,0:T(8,128)(2,1)S(1)} %get-tuple-element.191, bf16[768,3072]{1,0:T(8,128)(2,1)} %param.58), kind=kOutput, calls=%fused_computation.24 | convolution fusion | flops 4409524224 | bytes 33632256 | tf_op jit(solution)/shard_map/dot_general | solution.py:15
  246.2 13.0 fusion.13
  278.3 28.9 %multiply_reduce_fusion = (bf16[2,12,448]{2,1,0:T(8,128)(2,1)S(1)}, f32[2,12,448,750]{3,2,1,0:T(8,128)}) fusion(f32[2,12,448]{2,1,0:T(8,128)S(1)} %copy-done.54, f32[2,12,448]{2,1,0:T(8,128)S(1)} %copy-done.50, f32[2,12,448,750]{3,2,1,0:T(8,128)} %get-tuple-element.202, pred[2,750]{1,0:T(4,128)(4,1)S(1)} %copy-done.57, ...), kind=kOutput, calls=%fused_computation.2 | convolution fusion | flops 1072501248 | bytes 68301280 | tf_op jit(solution)/shard_map/tqhd,tkhd->thqk/dot_general | solution.py:67
  311.3 27.7 %multiply_convert_fusion = bf16[2,12,448,750]{3,2,1,0:T(8,128)(2,1)} fusion(f32[2,12,448,750]{3,2,1,0:T(8,128)} %get-tuple-element.208, f32[2,12,448]{2,1,0:T(8,128)} %sub.122, f32[2,12,448]{2,1,0:T(8,128)} %copy-done.53, f32[2,12,448]{2,1,0:T(8,128)} %copy-done.49, f32[2,12,448,750]{3,2,1,0:T(8,128)} %get-tuple-element.202, pred[2,750]{1,0:T(4,128)(4,1)S(1)} %copy-done.57), kind=kLoop, calls=%fused_computation.1 | loop fusion | flops 48384000 | bytes 80770528 | tf_op jit(solution)/shard_map/convert_element_type | solution.py:71
  338.9 11.5 fusion.68
  354.5 14.5 convert_reduce_fusion.1
  431.1 11.0 fusion.62
  452.7 15.8 multiply_reduce_fusion.1
  468.5 15.4 multiply_convert_fusion.1
  583.2 57.0 %reduce-scatter.23.cloned.1.call-done = f32[768,48]{0,1:T(8,128)} async-done(((f32[768,768]{0,1:T(8,128)}), f32[768,48]{0,1:T(8,128)}) %reduce-scatter.23.cloned.1.call-update) | async-done | bytes 147472 | tf_op jit(solution)/shard_map/reduce_scatter | solution.py:275
  641.7 130.8 %reduce-scatter.21.cloned.1.call-done = f32[768,48]{0,1:T(8,128)} async-done(((f32[768,768]{0,1:T(8,128)}), f32[768,48]{0,1:T(8,128)}) %reduce-scatter.21.cloned.1.call-update) | async-done | bytes 147472 | tf_op jit(solution)/shard_map/reduce_scatter | solution.py:274
  774.0 131.7 %reduce-scatter.19.cloned.1.call-done = f32[768,48]{0,1:T(8,128)} async-done(((f32[768,768]{0,1:T(8,128)}), f32[768,48]{0,1:T(8,128)}) %reduce-scatter.19.cloned.1.call-update) | async-done | bytes 147472 | tf_op jit(solution)/shard_map/reduce_scatter | solution.py:272
  907.3 130.9 %reduce-scatter.17.cloned.1.call-done = f32[768,48]{0,1:T(8,128)} async-done(((f32[768,768]{0,1:T(8,128)}), f32[768,48]{0,1:T(8,128)}) %reduce-scatter.17.cloned.1.call-update) | async-done | bytes 147472 | tf_op jit(solution)/shard_map/reduce_scatter | solution.py:268
  1039.8 131.7 %reduce-scatter.15.cloned.1.call-done = f32[768,48]{0,1:T(8,128)} async-done(((f32[768,768]{0,1:T(8,128)}), f32[768,48]{0,1:T(8,128)}) %reduce-scatter.15.cloned.1.call-update) | async-done | bytes 147472 | tf_op jit(solution)/shard_map/reduce_scatter | solution.py:266
  1173.0 130.9 %reduce-scatter.13.cloned.1.call-done = f32[768,48]{0,1:T(8,128)} async-done(((f32[768,768]{0,1:T(8,128)}), f32[768,48]{0,1:T(8,128)}) %reduce-scatter.13.cloned.1.call-update) | async-done | bytes 147472 | tf_op jit(solution)/shard_map/reduce_scatter | solution.py:265
  1305.5 131.6 %reduce-scatter.11.cloned.1.call-done = f32[768,48]{0,1:T(8,128)} async-done(((f32[768,768]{0,1:T(8,128)}), f32[768,48]{0,1:T(8,128)}) %reduce-scatter.11.cloned.1.call-update) | async-done | bytes 147472 | tf_op jit(solution)/shard_map/reduce_scatter | solution.py:263
  1438.6 174.2 %reduce-scatter.29.cloned.1.call-done = f32[3072,48]{0,1:T(8,128)} async-done(((f32[3072,768]{0,1:T(8,128)}), f32[3072,48]{0,1:T(8,128)}) %reduce-scatter.29.cloned.1.call-update) | async-done | bytes 589840 | tf_op jit(solution)/shard_map/reduce_scatter | solution.py:283
  1614.7 174.5 %reduce-scatter.27.cloned.1.call-done = f32[768,192]{0,1:T(8,128)} async-done(((f32[768,3072]{0,1:T(8,128)}), f32[768,192]{0,1:T(8,128)}) %reduce-scatter.27.cloned.1.call-update) | async-done | bytes 589840 | tf_op jit(solution)/shard_map/reduce_scatter | solution.py:281
  1801.0 74.6 %all-reduce.14 = (bf16[768]{0:T(1024)(128)(2,1)S(1)}, bf16[768]{0:T(1024)(128)(2,1)S(1)}, bf16[768]{0:T(1024)(128)(2,1)S(1)}, bf16[768]{0:T(1024)(128)(2,1)S(1)}...) all-reduce(f32[768]{0:T(1024)S(1)} %get-tuple-element.146, ...), channel_id=2, replica_groups=mesh['seq'=16,'frm'=2] {'seq'}, use_global_device_ids=true, to_apply=%region_25.26.clone | all-reduce | flops 13056 | bytes 78336
  (387 shorter events, 383.1 us)
Async XLA Ops:
  7.2 200.8 %all-reduce.21.cloned.1.call-start = ((), (), s32[]{:S(2)}) async-start(), calls=%async_computation.10 | async-start | bytes 2752512 | tf_op jit(solution)/shard_map/psum | solution.py:173
  9.1 31.8 %copy-start.60 = (f32[896]{0:T(1024)}, f32[896]{0:T(1024)S(1)}, u32[]{:S(2)}) copy-start(f32[896]{0:T(1024)S(1)} %div.60) | copy-start | bytes 10756
  11.9 29.0 %copy-start.62 = (f32[896]{0:T(1024)}, f32[896]{0:T(1024)S(1)}, u32[]{:S(2)}) copy-start(f32[896]{0:T(1024)S(1)} %rsqrt.28) | copy-start | bytes 10756
  127.3 40.6 %copy-start.56 = (pred[2,750]{1,0:T(4,128)(4,1)}, pred[2,750]{1,0:T(4,128)(4,1)S(1)}, u32[]{:S(2)}) copy-start(pred[2,750]{1,0:T(4,128)(4,1)S(1)} %broadcast_compare_fusion) | copy-start | bytes 4504
  147.2 20.8 %copy-start.45 = (bf16[2,750,12,64]{1,0,3,2:T(2,128)(2,1)S(1)}, bf16[2,750,12,64]{1,0,3,2:T(2,128)(2,1)}, u32[]{:S(2)}) copy-start(bf16[2,750,12,64]{1,0,3,2:T(2,128)(2,1)} %reshape.348) | copy-start | bytes 6912004
  185.2 217.1 %all-reduce.23.cloned.1.call-start = ((), (), s32[]{:S(2)}) async-start(), calls=%async_computation.11 | async-start | bytes 3145728 | tf_op jit(solution)/shard_map/psum | solution.py:218
  188.9 57.3 %copy-start.39 = (bf16[896,768]{1,0:T(8,128)(2,1)}, bf16[896,768]{1,0:T(8,128)(2,1)S(1)}, u32[]{:S(2)}) copy-start(bf16[896,768]{1,0:T(8,128)(2,1)S(1)} %bitcast_convert_fusion) | copy-start | bytes 4128772
  214.9 31.3 %copy-start.42 = (bf16[896,768]{1,0:T(8,128)(2,1)}, bf16[896,768]{1,0:T(8,128)(2,1)S(1)}, u32[]{:S(2)}) copy-start(bf16[896,768]{1,0:T(8,128)(2,1)S(1)} %get-tuple-element.191) | copy-start | bytes 4128772
  311.2 27.7 %copy-start.9 = (bf16[2,750,12,64]{1,0,3,2:T(2,128)(2,1)S(1)}, bf16[2,750,12,64]{1,0,3,2:T(2,128)(2,1)}, u32[]{:S(2)}) copy-start(bf16[2,750,12,64]{1,0,3,2:T(2,128)(2,1)} %reshape.350) | copy-start | bytes 6912004
  350.4 231.1 %reduce-scatter.25.cloned.1.call-start = ((), (), s32[]{:S(2)}) async-start(), calls=%async_computation.19 | async-start | bytes 2506752 | tf_op jit(solution)/shard_map/reduce_scatter | solution.py:277
  354.4 285.8 %reduce-scatter.23.cloned.1.call-start = ((), (), s32[]{:S(2)}) async-start(), calls=%async_computation.18 | async-start | bytes 2506752 | tf_op jit(solution)/shard_map/reduce_scatter | solution.py:275
  380.5 392.0 %reduce-scatter.21.cloned.1.call-start = ((), (), s32[]{:S(2)}) async-start(), calls=%async_computation.17 | async-start | bytes 2506752 | tf_op jit(solution)/shard_map/reduce_scatter | solution.py:274
  402.2 503.5 %reduce-scatter.19.cloned.1.call-start = ((), (), s32[]{:S(2)}) async-start(), calls=%async_computation.16 | async-start | bytes 2506752 | tf_op jit(solution)/shard_map/reduce_scatter | solution.py:272
  414.3 623.9 %reduce-scatter.17.cloned.1.call-start = ((), (), s32[]{:S(2)}) async-start(), calls=%async_computation.15 | async-start | bytes 2506752 | tf_op jit(solution)/shard_map/reduce_scatter | solution.py:268
  423.2 748.3 %reduce-scatter.15.cloned.1.call-start = ((), (), s32[]{:S(2)}) async-start(), calls=%async_computation.14 | async-start | bytes 2506752 | tf_op jit(solution)/shard_map/reduce_scatter | solution.py:266
  452.6 851.3 %reduce-scatter.13.cloned.1.call-start = ((), (), s32[]{:S(2)}) async-start(), calls=%async_computation.13 | async-start | bytes 2506752 | tf_op jit(solution)/shard_map/reduce_scatter | solution.py:265
  503.5 933.5 %reduce-scatter.11.cloned.1.call-start = ((), (), s32[]{:S(2)}) async-start(), calls=%async_computation.12 | async-start | bytes 2506752 | tf_op jit(solution)/shard_map/reduce_scatter | solution.py:263
  521.0 1091.9 %reduce-scatter.29.cloned.1.call-start = ((), (), s32[]{:S(2)}) async-start(), calls=%async_computation.21 | async-start | bytes 10027008 | tf_op jit(solution)/shard_map/reduce_scatter | solution.py:283
  529.3 1259.9 %reduce-scatter.27.cloned.1.call-start = ((), (), s32[]{:S(2)}) async-start(), calls=%async_computation.20 | async-start | bytes 10027008 | tf_op jit(solution)/shard_map/reduce_scatter | solution.py:281
  538.7 1351.8 %all-reduce.25.cloned.1.call-start = ((), (), s32[]{:S(2)}) async-start(), calls=%async_computation.22 | async-start | bytes 2359296 | tf_op jit(solution)/shard_map/psum | solution.py:288
  581.5 1209.5 %copy-start.3 = (bf16[2,448,768]{2,1,0:T(8,128)(2,1)S(1)}, bf16[2,448,768]{2,1,0:T(8,128)(2,1)}, u32[]{:S(2)}) copy-start(bf16[2,448,768]{2,1,0:T(8,128)(2,1)} %param.31) | copy-start | bytes 4128772
  581.5 1209.5 %copy-start.61 = (f32[896]{0:T(1024)S(1)}, f32[896]{0:T(1024)}, u32[]{:S(2)}) copy-start(f32[896]{0:T(1024)} %copy-done.60) | copy-start | bytes 10756
  581.5 1209.5 %copy-start.63 = (f32[896]{0:T(1024)S(1)}, f32[896]{0:T(1024)}, u32[]{:S(2)}) copy-start(f32[896]{0:T(1024)} %copy-done.62) | copy-start | bytes 10756
  581.5 1209.5 %copy-start.67 = (f32[768]{0:T(1024)S(1)}, f32[768]{0:T(1024)}, u32[]{:S(2)}) copy-start(f32[768]{0:T(1024)} %param.38) | copy-start | bytes 9220
  (84 other events, 423.7 us)
Sparse Core Ops, SparseCore 0:
  185.3 22.6 all-reduce.20
  350.6 21.6 all-reduce.22
  377.2 129.7 reduce-scatter.24
  512.5 127.6 reduce-scatter.22
  644.9 127.5 reduce-scatter.20
  778.0 127.6 reduce-scatter.18
  910.6 127.5 reduce-scatter.16
  1043.9 127.5 reduce-scatter.14
  1176.4 127.4 reduce-scatter.12
  1309.4 127.6 reduce-scatter.10
  1442.8 170.0 reduce-scatter.28
  1619.3 169.7 reduce-scatter.26
  1794.6 19.8 all-reduce.24
where the time goes:
time: 1920 us; the launch traced here: 1910 us
  waiting for transfers between devices  1210 us (63%)
  matrix products  326 us (17%)
  local copies, waits for them, and re-layouts  139 us (7%)
  other arithmetic  127 us (7%)
  blocking collectives  89.9 us (5%)
    reduce_scatter x1, waiting for transfers between devices, shards(): lax.psum_scatter(grad_expand_weight, 'seq', scatter_dimension=1, tiled=True)  175 us
    reduce_scatter x1, waiting for transfers between devices, shards(): lax.psum_scatter(grad_shrink_weight, 'seq', scatter_dimension=1, tiled=True)  174 us
    reduce_scatter x1, waiting for transfers between devices, shards(): lax.psum_scatter(grad_self_value, 'seq', scatter_dimension=1, tiled=True)  132 us
    reduce_scatter x1, waiting for transfers between devices, shards(): lax.psum_scatter(grad_cross_query, 'seq', scatter_dimension=1, tiled=True)  132 us
    reduce_scatter x1, waiting for transfers between devices, shards(): lax.psum_scatter(grad_self_query, 'seq', scatter_dimension=1, tiled=True)  132 us
    reduce_scatter x1, waiting for transfers between devices, shards(): lax.psum_scatter(grad_self_out, 'seq', scatter_dimension=1, tiled=True)  131 us
    reduce_scatter x1, waiting for transfers between devices, shards(): lax.psum_scatter(grad_self_key, 'seq', scatter_dimension=1, tiled=True)  131 us
    reduce_scatter x1, waiting for transfers between devices, shards(): lax.psum_scatter(grad_cross_key, 'seq', scatter_dimension=1, tiled=True)  131 us
  transfers between devices with their start and end apart: 13, of which 10 were waited for; matrix products, arithmetic and copies ran while one was open for 14% of the time, Pallas kernels for 0%

commit v1 on v0

v1 whole, which is shorter than its diff:
```python
import jax
import jax.numpy as jnp
from jax import lax
from jax.sharding import PartitionSpec as P

HEADS = 12
HDIM = 64
BF16 = jnp.bfloat16
F32 = jnp.float32


def matmul(left, right):
    return jnp.dot(left, right, preferred_element_type=F32)


def matmul_right_t(left, right):
    return lax.dot_general(left, right, (((1,), (1,)), ((), ())), preferred_element_type=F32)


def matmul_left_t(left, right):
    return lax.dot_general(left, right, (((0,), (0,)), ((), ())), preferred_element_type=F32)


def normalize(value, gain, shift):
    center = jnp.mean(value, axis=-1, keepdims=True)
    centered = value - center
    rstd = lax.rsqrt(jnp.mean(centered * centered, axis=-1, keepdims=True) + 1e-05)
    unit = centered * rstd
    return (unit * gain + shift, unit, rstd)


def normalize_back(grad, unit, rstd, gain):
    scaled = grad * gain
    return rstd * (
        scaled
        - jnp.mean(scaled, axis=-1, keepdims=True)
        - unit * jnp.mean(scaled * unit, axis=-1, keepdims=True)
    )


def heads_view(value):
    return value.reshape(value.shape[0], HEADS, HDIM)


def attention_scores(queries, key_rows, key_mask):
    scores = jnp.einsum("qhd,khd->hqk", queries, key_rows, preferred_element_type=F32)
    return jnp.where(key_mask, scores, -1e30)


def local_softmax(scores):
    row_top = jnp.max(scores, axis=-1, keepdims=True)
    weights = jnp.exp(scores - row_top)
    return weights / jnp.sum(weights, axis=-1, keepdims=True)


def attention_back(probs, dmix, value_rows, queries, key_rows):
    probs_low = probs.astype(BF16)
    dprob = jnp.einsum("qhd,khd->hqk", dmix, value_rows, preferred_element_type=F32)
    inner = jnp.sum(probs * dprob, axis=-1, keepdims=True)
    dscore = (probs * (dprob - inner)).astype(BF16)
    dquery = jnp.einsum("hqk,khd->qhd", dscore, key_rows, preferred_element_type=F32)
    dkeys = jnp.einsum("hqk,qhd->khd", dscore, queries, preferred_element_type=F32)
    dvalues = jnp.einsum("hqk,qhd->khd", probs_low, dmix, preferred_element_type=F32)
    flat = lambda v: v.astype(BF16).reshape(v.shape[0], -1)
    return flat(dquery), flat(dkeys), flat(dvalues)


def exact_gelu(value):
    return jax.nn.gelu(value, approximate=False)


class Links:
    def __init__(self):
        self.chips = lax.axis_size("seq")
        self.halving = self.chips == 16
        self.core = lax.axis_index("frm")
        self.chip = lax.axis_index("seq")

    def move(self, value, where):
        pairs = []
        for chip in range(self.chips):
            for core in range(2):
                to_chip, to_core = where(chip, core)
                pairs.append((chip * 2 + core, to_chip * 2 + to_core))
        return lax.ppermute(value, ("seq", "frm"), pairs)

    def swap(self, value):
        return self.move(value, lambda chip, core: (chip, 1 - core))

    def order(self, core):
        first = 1 + core
        second = 3 - first
        plane = jnp.stack([jnp.int32(0) * core, second, first, jnp.int32(3) + 0 * core])
        plane = plane ^ (self.chip % 4)
        along = jnp.arange(4) ^ (self.chip // 4)
        return (along[None, :] * 4 + plane[:, None]).reshape(16)

    def reduce(self, grads):
        if not self.halving:
            return [
                lax.psum(
                    lax.psum_scatter(g, "seq", scatter_dimension=0, tiled=True).astype(BF16), "frm"
                ).astype(F32)
                for g in grads
            ]
        mine, theirs = [], []
        for g in grads:
            half = g.shape[1] // 2
            cut = g.astype(BF16).reshape(16, g.shape[0] // 16, g.shape[1])
            for core, out in ((self.core, mine), (1 - self.core, theirs)):
                part = lax.dynamic_slice_in_dim(cut, core * half, half, 2)
                out.append(jnp.take(part, self.order(core), axis=0))
        add = lambda a, b: (a.astype(F32) + b.astype(F32)).astype(BF16)
        got = [self.swap(t) for t in theirs]
        keep = [add(m[:8], t[:8]) for m, t in zip(mine, got)]
        send = [add(m[8:], t[8:]) for m, t in zip(mine, got)]
        got = [self.move(s, lambda chip, core: (chip ^ (1 + core), core)) for s in send]
        send = [add(k[4:], t[4:]) for k, t in zip(keep, got)]
        keep = [add(k[:4], t[:4]) for k, t in zip(keep, got)]
        got = [self.move(s, lambda chip, core: (chip ^ (2 - core), core)) for s in send]
        parts = [[add(k[i], t[i]) for i in range(4)] for k, t in zip(keep, got)]
        totals = []
        for p in parts:
            total = p[0].astype(F32)
            for i in (1, 2, 3):
                arrived = self.move(p[i], lambda chip, core, i=i: (chip ^ (4 * i), core))
                total = total + arrived.astype(F32)
            totals.append(total.astype(BF16))
        outs = []
        for total in totals:
            other = self.swap(total)
            first = jnp.where(self.core == 0, total, other)
            second = jnp.where(self.core == 0, other, total)
            outs.append(jnp.concatenate([first, second], axis=1).astype(F32))
        return outs

    def reduce_vectors(self, vectors):
        if not self.halving:
            return [
                lax.psum(
                    lax.psum_scatter(v, "seq", scatter_dimension=0, tiled=True).astype(BF16), "frm"
                ).astype(F32)
                for v in vectors
            ]
        widths = [v.shape[0] // 16 for v in vectors]
        packed = jnp.concatenate([v.reshape(16, -1) for v in vectors], axis=1)
        packed = jnp.pad(packed, ((0, 0), (0, -packed.shape[1] % 1024))).reshape(16, 8, -1)
        packed = jnp.take(packed, self.order(jnp.int32(0)), axis=0)
        packed = packed + self.swap(packed)
        packed = packed[:8] + self.move(packed[8:], lambda chip, core: (chip ^ 1, core))
        packed = packed[:4] + self.move(packed[4:], lambda chip, core: (chip ^ 2, core))
        total = packed[0]
        for i in (1, 2, 3):
            total = total + self.move(packed[i], lambda chip, core, i=i: (chip ^ (4 * i), core))
        total = total.reshape(-1)
        outs, at = [], 0
        for width in widths:
            outs.append(total[at : at + width])
            at += width
        return outs


def shards(
    hidden,
    encoder,
    cotangent,
    lengths,
    frame_counts,
    corpus_ids,
    corpus_weights,
    first_gain,
    first_shift,
    self_query,
    self_query_bias,
    self_key,
    self_value,
    self_value_bias,
    self_out,
    self_out_bias,
    second_gain,
    second_shift,
    cross_query,
    cross_query_bias,
    cross_key,
    cross_value,
    cross_value_bias,
    cross_out,
    cross_out_bias,
    third_gain,
    third_shift,
    expand_weight,
    expand_bias,
    shrink_weight,
    shrink_bias,
):
    links = Links()
    core = links.core
    num_slots, width = hidden.shape[1:]
    local_frames = encoder.shape[1]
    pad_frames = -local_frames % 128
    block = local_frames + pad_frames
    scale = HDIM ** (-0.5)
    scale_low = jnp.asarray(scale, BF16)
    pick = lambda value, index: lax.dynamic_index_in_dim(value, index, 0, keepdims=False)
    length = pick(lengths, core)
    frame_total = pick(frame_counts, core)
    corpus = pick(corpus_ids, core)
    row_scale = jnp.sum(
        jnp.where(jnp.arange(corpus_weights.shape[0]) == corpus, corpus_weights, 0.0)
    )
    own_states = pick(encoder, core)
    far_states = links.swap(pick(encoder, 1 - core))
    padding = ((0, pad_frames), (0, 0))
    states = jnp.concatenate([jnp.pad(own_states, padding), jnp.pad(far_states, padding)])
    place = jnp.arange(2 * block)
    in_half = place % block
    half = jnp.where(place < block, core, 1 - core)
    frame_live = (in_half < local_frames) & (half * local_frames + in_half < frame_total)

    slot_index = jnp.arange(num_slots)
    self_mask = (slot_index[:, None] >= slot_index[None, :]) & (slot_index[None, :] < length)
    inputs = pick(hidden, core).astype(F32)
    normed_one, unit_one, rstd_one = normalize(inputs, first_gain, first_shift)
    low_one = normed_one.astype(BF16)
    queries = heads_view(((matmul(low_one, self_query) + self_query_bias) * scale).astype(BF16))
    key_rows = heads_view(matmul(low_one, self_key).astype(BF16))
    value_rows = heads_view((matmul(low_one, self_value) + self_value_bias).astype(BF16))
    probs = local_softmax(attention_scores(queries, key_rows, self_mask[None]))
    weigh = lambda p, v: jnp.einsum(
        "hqk,khd->qhd", p.astype(BF16), v, preferred_element_type=F32
    ).astype(BF16).reshape(num_slots, width)
    mixture = weigh(probs, value_rows)
    after_self = inputs + matmul(mixture, self_out) + self_out_bias
    normed_two, unit_two, rstd_two = normalize(after_self, second_gain, second_shift)
    low_two = normed_two.astype(BF16)
    cross_queries = heads_view(
        ((matmul(low_two, cross_query) + cross_query_bias) * scale).astype(BF16)
    )
    cross_keys = heads_view(matmul(states, cross_key).astype(BF16))
    cross_values = heads_view((matmul(states, cross_value) + cross_value_bias).astype(BF16))
    cross_probs = local_softmax(
        attention_scores(cross_queries, cross_keys, frame_live[None, None, :])
    )
    cross_mixture = weigh(cross_probs, cross_values)
    after_cross = after_self + matmul(cross_mixture, cross_out) + cross_out_bias
    normed_three, unit_three, rstd_three = normalize(after_cross, third_gain, third_shift)
    low_three = normed_three.astype(BF16)
    pre_active = matmul(low_three, expand_weight) + expand_bias
    active, gelu_back = jax.vjp(exact_gelu, pre_active)
    active_low = active.astype(BF16)
    result = after_cross + matmul(active_low, shrink_weight) + shrink_bias
    output = result.astype(BF16)

    live_rows = (slot_index < length).astype(F32) * row_scale
    grad_result = pick(cotangent, core).astype(F32) * live_rows[:, None]
    dshrink = grad_result.astype(BF16)
    column_sum = lambda v: jnp.sum(v.astype(F32), axis=0)
    dactive = matmul_right_t(dshrink, shrink_weight).astype(BF16)
    dpre = gelu_back(dactive.astype(F32))[0].astype(BF16)
    feed_grads = links.reduce([matmul_left_t(dpre, low_three), matmul_left_t(dshrink, active_low)])
    dnormed_three = matmul_right_t(dpre, expand_weight)
    dafter_cross = grad_result + normalize_back(dnormed_three, unit_three, rstd_three, third_gain)
    dcross = dafter_cross.astype(BF16)
    dcross_mix = heads_view(matmul_right_t(dcross, cross_out).astype(BF16))
    dcq, dck_rows, dcv_rows = attention_back(
        cross_probs, dcross_mix, cross_values, cross_queries, cross_keys
    )
    dcq_scaled = dcq * scale_low
    cross_grads = links.reduce(
        [
            matmul_left_t(dcq_scaled, low_two),
            matmul_left_t(dck_rows, states),
            matmul_left_t(dcv_rows, states),
            matmul_left_t(dcross, cross_mixture),
        ]
    )
    dnormed_two = matmul_right_t(dcq_scaled, cross_query)
    grad_states = matmul_right_t(dck_rows, cross_key) + matmul_right_t(dcv_rows, cross_value)
    dafter_self = dafter_cross + normalize_back(dnormed_two, unit_two, rstd_two, second_gain)
    dself = dafter_self.astype(BF16)
    dself_mix = heads_view(matmul_right_t(dself, self_out).astype(BF16))
    dquery, dkey_rows, dvalue_rows = attention_back(
        probs, dself_mix, value_rows, queries, key_rows
    )
    dquery_scaled = dquery * scale_low
    self_grads = links.reduce(
        [
            matmul_left_t(dquery_scaled, low_one),
            matmul_left_t(dkey_rows, low_one),
            matmul_left_t(dvalue_rows, low_one),
            matmul_left_t(dself, mixture),
        ]
    )
    dnormed_one = (
        matmul_right_t(dquery_scaled, self_query)
        + matmul_right_t(dkey_rows, self_key)
        + matmul_right_t(dvalue_rows, self_value)
    )
    grad_inputs = dafter_self + normalize_back(dnormed_one, unit_one, rstd_one, first_gain)
    vectors = links.reduce_vectors(
        [
            column_sum(dnormed_one * unit_one),
            column_sum(dnormed_one),
            column_sum(dquery_scaled),
            column_sum(dvalue_rows),
            column_sum(dself),
            column_sum(dnormed_two * unit_two),
            column_sum(dnormed_two),
            column_sum(dcq_scaled),
            column_sum(dcv_rows),
            column_sum(dcross),
            column_sum(dnormed_three * unit_three),
            column_sum(dnormed_three),
            column_sum(dpre),
            column_sum(dshrink),
        ]
    )

    def both(own):
        far = links.swap(own)
        return jnp.stack([jnp.where(core == 0, own, far), jnp.where(core == 0, far, own)])

    own_half = grad_states[:local_frames].astype(BF16)
    far_half = links.swap(grad_states[block : block + local_frames].astype(BF16))
    grad_encoder = jnp.stack(
        [jnp.where(core == 0, own_half, far_half), jnp.where(core == 0, far_half, own_half)]
    ).astype(F32)
    t = jnp.transpose
    return (
        both(output),
        both(grad_inputs.astype(BF16)).astype(F32),
        grad_encoder,
        vectors[0],
        vectors[1],
        t(self_grads[0]),
        vectors[2],
        t(self_grads[1]),
        t(self_grads[2]),
        vectors[3],
        t(self_grads[3]),
        vectors[4],
        vectors[5],
        vectors[6],
        t(cross_grads[0]),
        vectors[7],
        t(cross_grads[1]),
        t(cross_grads[2]),
        vectors[8],
        t(cross_grads[3]),
        vectors[9],
        vectors[10],
        vectors[11],
        t(feed_grads[0]),
        vectors[12],
        t(feed_grads[1]),
        vectors[13],
    )


def solution(mesh):
    copied = P()
    return jax.shard_map(
        shards,
        mesh=mesh,
        in_specs=(
            P("seq", None, None),
            P("seq", "frm", None),
            P("seq", None, None),
            P("seq"),
            P("seq"),
            P("seq"),
        )
        + (copied,) * 25,
        out_specs=(P("seq", None, None), P("seq", None, None), P("seq", "frm", None))
        + tuple(
            P(None, "seq") if matrix else P("seq")
            for matrix in (0, 0, 1, 0, 1, 1, 0, 1, 0, 0, 0, 1, 0, 1, 1, 0, 1, 0, 0, 0, 1, 0, 1, 0)
        ),
        check_vma=False,
    )
```

time: 1920 us -> 625 us (0.33)
  waiting for transfers between devices: 1210 us -> 85.3 us
  matrix products: 326 us -> 231 us
  blocking collectives: 89.9 us -> 0 us
  starting transfers between devices: 0.92 us -> 87.3 us
  other arithmetic: 127 us -> 74.7 us
    reduce_scatter x10 -> x0, waiting for transfers between devices: 1190 us -> none  [the longest x1 175 us: shards(): lax.psum_scatter(grad_expand_weight, 'seq', scatter_dimension=1, tiled=True)]
    ppermute x0 -> x80, starting transfers between devices: none -> 87.3 us  [move(): return lax.ppermute(value, ('seq', 'frm'), pairs)]
    ppermute x0 -> x80, waiting for transfers between devices: none -> 85.3 us  [move(): return lax.ppermute(value, ('seq', 'frm'), pairs)]
    unnamed x1 -> x0, blocking collectives: 74.6 us -> none
    dot_general x21 -> x20, matrix products: 212 us -> 140 us  [the longest x10 44.1 us: matmul(): return jnp.dot(left, right, preferred_element_type=F32)]
    gather x0 -> x21, local copies, waits for them, and re-layouts: none -> 57.6 us  [the longest x20 55.4 us: reduce(): out.append(jnp.take(part, self.order(core), axis=0))]
    convert_element_type x20 -> x6, local copies, waits for them, and re-layouts: 58 us -> 7.17 us  [the longest x1 1.4 us: shards(): key_rows = heads_view(matmul(low_one, self_key).astype(BF16))]
    convert_element_type x41 -> x45, other arithmetic: 90.3 us -> 40.7 us  [the longest x2 30.5 us: attention_back(): dscore = (probs * (dprob - inner)).astype(BF16)]
  transfers between devices with their start and end apart: 13 -> 80, of which waited for: 10 -> 38; matrix products, arithmetic and copies ran while one was open for 14% -> 33% of each run, Pallas kernels for 0% -> 0%
where the time goes in v1:
time: 625 us; the launch traced here: 616 us
  matrix products  231 us (37%)
  local copies, waits for them, and re-layouts  135 us (22%)
  starting transfers between devices  87.3 us (14%)
  waiting for transfers between devices  85.3 us (14%)
  other arithmetic  74.7 us (12%)
    ppermute x80, starting transfers between devices, move(): return lax.ppermute(value, ('seq', 'frm'), pairs)  87.3 us
    ppermute x80, waiting for transfers between devices, move(): return lax.ppermute(value, ('seq', 'frm'), pairs)  85.3 us
    gather x20, local copies, waits for them, and re-layouts, reduce(): out.append(jnp.take(part, self.order(core), axis=0))  55.4 us
    dot_general x10, matrix products, matmul(): return jnp.dot(left, right, preferred_element_type=F32)  44.1 us
    dot_general x10, matrix products, matmul_right_t(): lax.dot_general(left, right, (((1,), (1,)), ((), ())), preferred_element_...  37.1 us
    dot_general x2, matrix products, attention_back(): jnp.einsum('qhd,khd->hqk', dmix, value_rows, preferred_element_type=F32)  30.6 us
    convert_element_type x2, other arithmetic, attention_back(): dscore = (probs * (dprob - inner)).astype(BF16)  30.5 us
    dot_general x10, matrix products, matmul_left_t(): lax.dot_general(left, right, (((0,), (0,)), ((), ())), preferred_element_...  28.2 us
  transfers between devices with their start and end apart: 80, of which 38 were waited for; matrix products, arithmetic and copies ran while one was open for 33% of the time, Pallas kernels for 0%

profile of v1, /device:TPU:0, one launch (start us, length us, event | category | flops | bytes accessed | tf_op | source)
XLA Modules:
  0.0 615.7 jit_solution(15088208635605320355)
XLA Ops:
  0.7 8.6 %constant_dynamic-slice_fusion.21 = (bf16[1,750,768]{2,0,1:T(2,128)(2,1)}, bf16[1,750,768]{2,0,1:T(2,128)(2,1)S(1)}) fusion(bf16[2,750,768]{2,0,1:T(2,128)(2,1)} %param.38, s32[]{:T(128)S(6)} %select_n.308, s32[]{:T(128)S(6)} %select_n.310), kind=kLoop, calls=%fused_computation.427 | loop fusion | bytes 4608008 | tf_op jit(solution)/shard_map/jit(dynamic_index_in_dim)/dynamic_slice | solution.py:204
  26.7 8.2 %fusion.193 = (f32[12,448]{1,0:T(8,128)}, f32[12,448,448]{1,2,0:T(8,128)}) fusion(pred[448,448]{0,1:T(8,128)(4,1)} %fusion.84, bf16[448,12,64]{0,2,1:T(8,128)(2,1)S(1)} %bitcast.354, bf16[448,12,64]{0,2,1:T(8,128)(2,1)S(1)} %bitcast.356), kind=kOutput, calls=%fused_computation.484 | convolution fusion | flops 315507136 | bytes 11232256 | tf_op jit(solution)/shard_map/sub | solution.py:52
  35.0 5.3 fusion.56
  57.3 5.1 convolution_convert_fusion.3
  62.4 16.6 %fusion.195 = (f32[12,448]{1,0:T(8,128)S(1)}, f32[12,448,1536]{2,1,0:T(8,128)}) fusion(pred[1536]{0:T(1024)(128)(4,1)S(1)} %fusion.159, bf16[448,12,64]{0,2,1:T(8,128)(2,1)S(1)} %bitcast.348, bf16[1536,12,64]{0,2,1:T(8,128)(2,1)} %bitcast.360), kind=kOutput, calls=%fused_computation.486 | convolution fusion | flops 1081738752 | bytes 36100608 | tf_op jit(solution)/shard_map/sub | solution.py:52
  79.0 5.4 add_convert_fusion.1
  84.4 13.7 %fusion.53 = bf16[12,64,448]{2,1,0:T(8,128)(2,1)S(1)} fusion(bf16[1536,12,64]{0,2,1:T(8,128)(2,1)} %bitcast.389, f32[12,448,1536]{2,1,0:T(8,128)} %get-tuple-element.261, f32[12,448]{1,0:T(8,128)S(1)} %get-tuple-element.260), kind=kOutput, calls=%fused_computation.129 | convolution fusion | flops 1073823744 | bytes 36099072 | tf_op jit(solution)/shard_map/hqk,khd->qhd/dot_general | solution.py:229
  101.4 17.0 %multiply_convert_fusion.2 = (bf16[448,3072]{1,0:T(8,128)(2,1)}, f32[448,3072]{1,0:T(8,128)S(1)}, f32[448,3072]{1,0:T(8,128)S(1)}) fusion(f32[3072]{0:T(1024)S(1)} %copy-done.82, bf16[768,3072]{1,0:T(8,128)(2,1)} %param.64, f32[448,768]{1,0:T(8,128)S(1)} %get-tuple-element.263, f32[768]{0:T(1024)S(1)} %copy-done.88, f32[768]{0:T(1024)S(1)} %copy-done.73, ...), kind=kOutput, calls=%fused_computation.52 | convolution fusion | flops 2206482432 | bytes 19879424 | tf_op jit(solution)/shard_map/dot_general | solution.py:13
  118.4 7.5 %convert_reduce_fusion = (f32[3072]{0:T(1024)}, bf16[448,3072]{1,0:T(8,128)(2,1)S(1)}) fusion(f32[448,3072]{1,0:T(8,128)S(1)} %get-tuple-element.101, bf16[3072,768]{1,0:T(8,128)(2,1)} %param.66, f32[448]{0:T(512)S(1)} %broadcast_select_fusion.41, bf16[2,448,768]{2,1,0:T(8,128)(2,1)S(1)} %copy-done.49, s32[]{:T(128)S(6)} %select_n.308, ...), kind=kOutput, calls=%fused_computation.51 | convolution fusion | flops 2141107200 | bytes 19195908 | tf_op jit(solution)/shard_map/dot_general | solution.py:17
  130.5 5.6 multiply_reduce_fusion.2
  139.5 25.1 %multiply_reduce_fusion = (f32[12,448]{1,0:T(8,128)S(1)}, f32[12,448,1536]{2,1,0:T(8,128)}) fusion(f32[12,448,1536]{2,1,0:T(8,128)} %get-tuple-element.261, f32[12,448]{1,0:T(8,128)S(1)} %get-tuple-element.260, bf16[448,12,64]{0,2,1:T(8,128)(2,1)S(1)} %bitcast.380, bf16[1536,12,64]{0,2,1:T(8,128)(2,1)} %bitcast.390), kind=kOutput, calls=%fused_computation.24 | convolution fusion | flops 1081731840 | bytes 69150720 | tf_op jit(solution)/shard_map/qhd,khd->hqk/dot_general | solution.py:58
  164.7 14.2 %convert_reduce_fusion.1 = (f32[12,64]{1,0:T(8,128)}, bf16[12,64,1536]{2,1,0:T(8,128)(2,1)}) fusion(bf16[448,12,64]{0,2,1:T(8,128)(2,1)S(1)} %bitcast.381, f32[12,448,1536]{2,1,0:T(8,128)} %get-tuple-element.261, f32[12,448]{1,0:T(8,128)S(1)} %get-tuple-element.260), kind=kOutput, calls=%fused_computation.73 | convolution fusion | flops 1077017856 | bytes 36102144 | tf_op jit(solution)/shard_map/hqk,qhd->khd/dot_general | solution.py:63
  178.8 27.3 %multiply_convert_fusion = bf16[12,448,1536]{2,1,0:T(8,128)(2,1)} fusion(f32[12,448,1536]{2,1,0:T(8,128)} %get-tuple-element.267, f32[12,448]{1,0:T(8,128)S(1)} %get-tuple-element.266, f32[12,448,1536]{2,1,0:T(8,128)} %get-tuple-element.261, f32[12,448]{1,0:T(8,128)S(1)} %get-tuple-element.260), kind=kLoop, calls=%fused_computation.23 | loop fusion | flops 33030144 | bytes 82618368 | tf_op jit(solution)/shard_map/convert_element_type | solution.py:60
  206.2 11.3 %convert_reduce_fusion.3 = (f32[12,64]{1,0:T(8,128)S(1)}, bf16[12,64,448]{2,1,0:T(8,128)(2,1)S(1)}) fusion(bf16[1536,12,64]{0,2,1:T(8,128)(2,1)} %bitcast.361, bf16[12,448,1536]{2,1,0:T(8,128)(2,1)} %multiply_convert_fusion), kind=kOutput, calls=%fused_computation.108 | convolution fusion | flops 1058340096 | bytes 19565568 | tf_op jit(solution)/shard_map/hqk,khd->qhd/dot_general | solution.py:61
  217.5 10.2 %convolution_convert_fusion.4 = bf16[12,64,1536]{2,1,0:T(8,128)(2,1)} fusion(bf16[448,12,64]{0,2,1:T(8,128)(2,1)S(1)} %bitcast.349, bf16[12,448,1536]{2,1,0:T(8,128)(2,1)} %multiply_convert_fusion), kind=kOutput, calls=%fused_computation.81 | convolution fusion | flops 1058144256 | bytes 19562496 | tf_op jit(solution)/shard_map/hqk,qhd->khd/dot_general | solution.py:62
  235.9 7.4 %convert_reduce_fusion.4 = (f32[12,64]{1,0:T(8,128)}, bf16[12,64,448]{2,1,0:T(8,128)(2,1)}) fusion(bf16[448,12,64]{0,2,1:T(8,128)(2,1)S(1)} %bitcast.382, f32[12,448,448]{1,2,0:T(8,128)} %get-tuple-element.257, f32[12,448]{1,0:T(8,128)S(1)} %copy-done.51), kind=kOutput, calls=%fused_computation.109 | convolution fusion | flops 314129664 | bytes 11034624 | tf_op jit(solution)/shard_map/hqk,qhd->khd/dot_general | solution.py:63
  243.3 5.5 multiply_reduce_fusion.1
  276.8 5.0 constant_dynamic-slice_fusion.3
  307.7 6.0 fusion.198
  404.1 5.9 add_convert_fusion
  548.5 10.7 %collective-permute-done.74 = bf16[8,48,1536]{2,1,0:T(8,128)(2,1)S(1)} collective-permute-done((bf16[8,48,1536]{2,1,0:T(8,128)(2,1)S(1)}, bf16[8,48,1536]{2,1,0:T(8,128)(2,1)S(1)}, u32[]{:S(2)}, u32[]{:S(2)}) %collective-permute-start.74) | collective-permute-done | bytes 1179680 | tf_op jit(solution)/shard_map/ppermute | solution.py:85
  561.2 16.9 %collective-permute-done.67 = bf16[8,192,384]{2,1,0:T(8,128)(2,1)S(1)} collective-permute-done((bf16[8,192,384]{2,1,0:T(8,128)(2,1)S(1)}, bf16[8,192,384]{2,1,0:T(8,128)(2,1)S(1)}, u32[]{:S(2)}, u32[]{:S(2)}) %collective-permute-start.67) | collective-permute-done | bytes 1179680 | tf_op jit(solution)/shard_map/ppermute | solution.py:85
  580.3 5.7 copy.87
  600.7 12.3 %collective-permute-done.70 = bf16[192,384]{1,0:T(8,128)(2,1)S(1)} collective-permute-done((bf16[192,384]{1,0:T(8,128)(2,1)S(1)}, bf16[192,384]{1,0:T(8,128)(2,1)S(1)}, u32[]{:S(2)}, u32[]{:S(2)}) %collective-permute-start.70) | collective-permute-done | bytes 147488 | tf_op jit(solution)/shard_map/ppermute | solution.py:85
  (583 shorter events, 356.2 us)
Async XLA Ops:
  10.4 46.8 %collective-permute-start = (bf16[750,768]{1,0:T(8,128)(2,1)}, bf16[750,768]{1,0:T(8,128)(2,1)}, u32[]{:S(2)}, u32[]{:S(2)}) collective-permute-start(bf16[750,768]{1,0:T(8,128)(2,1)} %bitcast.342), channel_id=1, source_target_pairs={{0,1},{1,0},{2,3},{3,2},{4,5},{5,4},{6,7},{7,6},{8,9},{9,8},{10,11... | collective-permute-start | bytes 3456008 | tf_op jit(solution)/shard_map/ppermute | solution.py:85
  276.3 264.2 %collective-permute-start.73 = (bf16[16,48,1536]{2,1,0:T(8,128)(2,1)}, bf16[16,48,1536]{2,1,0:T(8,128)(2,1)}, u32[]{:S(2)}, u32[]{:S(2)}) collective-permute-start(bf16[16,48,1536]{2,1,0:T(8,128)(2,1)} %broadcast_select_fusion), channel_id=1, source_target_pairs={{0,1},{1,0},{2,3},{3,2},{4,5},{5,4},{6,7},{7,6},{8,9},{9,8},{10,11... | collective-permute-start | bytes 7077896 | tf_op jit(solution)/shard_map/ppermute | solution.py:85
  374.3 61.7 %collective-permute-start.59 = (bf16[16,48,384]{2,1,0:T(8,128)(2,1)}, bf16[16,48,384]{2,1,0:T(8,128)(2,1)}, u32[]{:S(2)}, u32[]{:S(2)}) collective-permute-start(bf16[16,48,384]{2,1,0:T(8,128)(2,1)} %get-tuple-element.245), channel_id=1, source_target_pairs={{0,1},{1,0},{2,3},{3,2},{4,5},{5,4},{6,7},{7,6},{8,9},{9,8},{10,11... | collective-permute-start | bytes 1769480 | tf_op jit(solution)/shard_map/ppermute | solution.py:85
  403.5 12.3 %collective-permute-start.4 = (f32[16,8,128]{2,1,0:T(8,128)S(1)}, f32[16,8,128]{2,1,0:T(8,128)S(1)}, u32[]{:S(2)}, u32[]{:S(2)}) collective-permute-start(f32[16,8,128]{2,1,0:T(8,128)S(1)} %broadcast_select_fusion.40), channel_id=1, source_target_pairs={{0,1},{1,0},{2,3},{3,2},{4,5},{5,4},{6,7},{7,6},{8,9},{9,8},{10,11... | collective-permute-start | bytes 196616 | tf_op jit(solution)/shard_map/ppermute | solution.py:85
  431.0 115.5 %collective-permute-start.66 = (bf16[16,192,384]{2,1,0:T(8,128)(2,1)S(1)}, bf16[16,192,384]{2,1,0:T(8,128)(2,1)S(1)}, u32[]{:S(2)}, u32[]{:S(2)}) collective-permute-start(bf16[16,192,384]{2,1,0:T(8,128)(2,1)S(1)} %copy-done.31), channel_id=1, source_target_pairs={{0,1},{1,0},{2,3},{3,2},{4,5},{5,4},{6,7},{7,6},{8,9},{9,8},{10,11... | collective-permute-start | bytes 7077896 | tf_op jit(solution)/shard_map/ppermute | solution.py:85
  444.9 10.5 %collective-permute-start.46 = (bf16[8,48,384]{2,1,0:T(8,128)(2,1)S(1)}, bf16[8,48,384]{2,1,0:T(8,128)(2,1)S(1)}, u32[]{:S(2)}, u32[]{:S(2)}) collective-permute-start(bf16[8,48,384]{2,1,0:T(8,128)(2,1)S(1)} %get-tuple-element.138), channel_id=1, source_target_pairs={{0,2},{1,5},{2,0},{3,7},{4,6},{5,1},{6,4},{7,3},{8,10},{9,13},{10,... | collective-permute-start | bytes 884744 | tf_op jit(solution)/shard_map/ppermute | solution.py:85
  449.5 9.1 %collective-permute-start.39 = (bf16[8,48,384]{2,1,0:T(8,128)(2,1)S(1)}, bf16[8,48,384]{2,1,0:T(8,128)(2,1)S(1)}, u32[]{:S(2)}, u32[]{:S(2)}) collective-permute-start(bf16[8,48,384]{2,1,0:T(8,128)(2,1)S(1)} %get-tuple-element.142), channel_id=1, source_target_pairs={{0,2},{1,5},{2,0},{3,7},{4,6},{5,1},{6,4},{7,3},{8,10},{9,13},{10,... | collective-permute-start | bytes 884744 | tf_op jit(solution)/shard_map/ppermute | solution.py:85
  452.3 9.5 %collective-permute-start.32 = (bf16[8,48,384]{2,1,0:T(8,128)(2,1)S(1)}, bf16[8,48,384]{2,1,0:T(8,128)(2,1)S(1)}, u32[]{:S(2)}, u32[]{:S(2)}) collective-permute-start(bf16[8,48,384]{2,1,0:T(8,128)(2,1)S(1)} %get-tuple-element.146), channel_id=1, source_target_pairs={{0,2},{1,5},{2,0},{3,7},{4,6},{5,1},{6,4},{7,3},{8,10},{9,13},{10,... | collective-permute-start | bytes 884744 | tf_op jit(solution)/shard_map/ppermute | solution.py:85
  455.4 9.5 %collective-permute-start.25 = (bf16[8,48,384]{2,1,0:T(8,128)(2,1)S(1)}, bf16[8,48,384]{2,1,0:T(8,128)(2,1)S(1)}, u32[]{:S(2)}, u32[]{:S(2)}) collective-permute-start(bf16[8,48,384]{2,1,0:T(8,128)(2,1)S(1)} %get-tuple-element.150), channel_id=1, source_target_pairs={{0,2},{1,5},{2,0},{3,7},{4,6},{5,1},{6,4},{7,3},{8,10},{9,13},{10,... | collective-permute-start | bytes 884744 | tf_op jit(solution)/shard_map/ppermute | solution.py:85
  458.6 10.7 %collective-permute-start.18 = (bf16[8,48,384]{2,1,0:T(8,128)(2,1)S(1)}, bf16[8,48,384]{2,1,0:T(8,128)(2,1)S(1)}, u32[]{:S(2)}, u32[]{:S(2)}) collective-permute-start(bf16[8,48,384]{2,1,0:T(8,128)(2,1)S(1)} %get-tuple-element.154), channel_id=1, source_target_pairs={{0,2},{1,5},{2,0},{3,7},{4,6},{5,1},{6,4},{7,3},{8,10},{9,13},{10,... | collective-permute-start | bytes 884744 | tf_op jit(solution)/shard_map/ppermute | solution.py:85
  461.7 12.6 %collective-permute-start.11 = (bf16[8,48,384]{2,1,0:T(8,128)(2,1)S(1)}, bf16[8,48,384]{2,1,0:T(8,128)(2,1)S(1)}, u32[]{:S(2)}, u32[]{:S(2)}) collective-permute-start(bf16[8,48,384]{2,1,0:T(8,128)(2,1)S(1)} %get-tuple-element.158), channel_id=1, source_target_pairs={{0,2},{1,5},{2,0},{3,7},{4,6},{5,1},{6,4},{7,3},{8,10},{9,13},{10,... | collective-permute-start | bytes 884744 | tf_op jit(solution)/shard_map/ppermute | solution.py:85
  464.9 11.1 %collective-permute-start.61 = (bf16[4,48,384]{2,1,0:T(8,128)(2,1)S(1)}, bf16[4,48,384]{2,1,0:T(8,128)(2,1)S(1)}, u32[]{:S(2)}, u32[]{:S(2)}) collective-permute-start(bf16[4,48,384]{2,1,0:T(8,128)(2,1)S(1)} %get-tuple-element.162), channel_id=1, source_target_pairs={{0,4},{1,3},{2,6},{3,1},{4,0},{5,7},{6,2},{7,5},{8,12},{9,11},{10,... | collective-permute-start | bytes 442376 | tf_op jit(solution)/shard_map/ppermute | solution.py:85
  532.3 28.8 %collective-permute-start.3 = (bf16[750,768]{1,0:T(8,128)(2,1)S(1)}, bf16[750,768]{1,0:T(8,128)(2,1)S(1)}, u32[]{:S(2)}, u32[]{:S(2)}) collective-permute-start(bf16[750,768]{1,0:T(8,128)(2,1)S(1)} %slice.781), channel_id=1, source_target_pairs={{0,1},{1,0},{2,3},{3,2},{4,5},{5,4},{6,7},{7,6},{8,9},{9,8},{10,11... | collective-permute-start | bytes 3456008 | tf_op jit(solution)/shard_map/ppermute | solution.py:85
  542.9 16.3 %collective-permute-start.74 = (bf16[8,48,1536]{2,1,0:T(8,128)(2,1)S(1)}, bf16[8,48,1536]{2,1,0:T(8,128)(2,1)S(1)}, u32[]{:S(2)}, u32[]{:S(2)}) collective-permute-start(bf16[8,48,1536]{2,1,0:T(8,128)(2,1)S(1)} %get-tuple-element.103), channel_id=1, source_target_pairs={{0,2},{1,5},{2,0},{3,7},{4,6},{5,1},{6,4},{7,3},{8,10},{9,13},{10,... | collective-permute-start | bytes 3538952 | tf_op jit(solution)/shard_map/ppermute | solution.py:85
  547.2 30.9 %collective-permute-start.67 = (bf16[8,192,384]{2,1,0:T(8,128)(2,1)S(1)}, bf16[8,192,384]{2,1,0:T(8,128)(2,1)S(1)}, u32[]{:S(2)}, u32[]{:S(2)}) collective-permute-start(bf16[8,192,384]{2,1,0:T(8,128)(2,1)S(1)} %get-tuple-element.107), channel_id=1, source_target_pairs={{0,2},{1,5},{2,0},{3,7},{4,6},{5,1},{6,4},{7,3},{8,10},{9,13},{10,... | collective-permute-start | bytes 3538952 | tf_op jit(solution)/shard_map/ppermute | solution.py:85
  559.5 26.6 %collective-permute-start.75 = (bf16[4,48,1536]{2,1,0:T(8,128)(2,1)S(1)}, bf16[4,48,1536]{2,1,0:T(8,128)(2,1)S(1)}, u32[]{:S(2)}, u32[]{:S(2)}) collective-permute-start(bf16[4,48,1536]{2,1,0:T(8,128)(2,1)S(1)} %get-tuple-element.113), channel_id=1, source_target_pairs={{0,4},{1,3},{2,6},{3,1},{4,0},{5,7},{6,2},{7,5},{8,12},{9,11},{10,... | collective-permute-start | bytes 1769480 | tf_op jit(solution)/shard_map/ppermute | solution.py:85
  578.4 12.2 %collective-permute-start.68 = (bf16[4,192,384]{2,1,0:T(8,128)(2,1)S(1)}, bf16[4,192,384]{2,1,0:T(8,128)(2,1)S(1)}, u32[]{:S(2)}, u32[]{:S(2)}) collective-permute-start(bf16[4,192,384]{2,1,0:T(8,128)(2,1)S(1)} %get-tuple-element.115), channel_id=1, source_target_pairs={{0,4},{1,3},{2,6},{3,1},{4,0},{5,7},{6,2},{7,5},{8,12},{9,11},{10,... | collective-permute-start | bytes 1769480 | tf_op jit(solution)/shard_map/ppermute | solution.py:85
  586.1 8.8 %collective-permute-start.76 = (bf16[48,1536]{1,0:T(8,128)(2,1)S(1)}, bf16[48,1536]{1,0:T(8,128)(2,1)S(1)}, u32[]{:S(2)}, u32[]{:S(2)}) collective-permute-start(bf16[48,1536]{1,0:T(8,128)(2,1)S(1)} %get-tuple-element.123), channel_id=1, source_target_pairs={{0,8},{1,9},{2,10},{3,11},{4,12},{5,13},{6,14},{7,15},{8,0},{9,1},... | collective-permute-start | bytes 442376 | tf_op jit(solution)/shard_map/ppermute | solution.py:85
  586.2 14.3 %collective-permute-start.77 = (bf16[48,1536]{1,0:T(8,128)(2,1)S(1)}, bf16[48,1536]{1,0:T(8,128)(2,1)S(1)}, u32[]{:S(2)}, u32[]{:S(2)}) collective-permute-start(bf16[48,1536]{1,0:T(8,128)(2,1)S(1)} %get-tuple-element.125), channel_id=1, source_target_pairs={{0,16},{1,17},{2,18},{3,19},{4,20},{5,21},{6,22},{7,23},{8,24},{9,... | collective-permute-start | bytes 442376 | tf_op jit(solution)/shard_map/ppermute | solution.py:85
  589.4 11.1 %collective-permute-start.78 = (bf16[48,1536]{1,0:T(8,128)(2,1)S(1)}, bf16[48,1536]{1,0:T(8,128)(2,1)S(1)}, u32[]{:S(2)}, u32[]{:S(2)}) collective-permute-start(bf16[48,1536]{1,0:T(8,128)(2,1)S(1)} %get-tuple-element.124), channel_id=1, source_target_pairs={{0,24},{1,25},{2,26},{3,27},{4,28},{5,29},{6,30},{7,31},{8,16},{9,... | collective-permute-start | bytes 442376 | tf_op jit(solution)/shard_map/ppermute | solution.py:85
  590.7 10.0 %collective-permute-start.69 = (bf16[192,384]{1,0:T(8,128)(2,1)S(1)}, bf16[192,384]{1,0:T(8,128)(2,1)S(1)}, u32[]{:S(2)}, u32[]{:S(2)}) collective-permute-start(bf16[192,384]{1,0:T(8,128)(2,1)S(1)} %get-tuple-element.126), channel_id=1, source_target_pairs={{0,8},{1,9},{2,10},{3,11},{4,12},{5,13},{6,14},{7,15},{8,0},{9,1},... | collective-permute-start | bytes 442376 | tf_op jit(solution)/shard_map/ppermute | solution.py:85
  590.8 22.2 %collective-permute-start.70 = (bf16[192,384]{1,0:T(8,128)(2,1)S(1)}, bf16[192,384]{1,0:T(8,128)(2,1)S(1)}, u32[]{:S(2)}, u32[]{:S(2)}) collective-permute-start(bf16[192,384]{1,0:T(8,128)(2,1)S(1)} %get-tuple-element.128), channel_id=1, source_target_pairs={{0,16},{1,17},{2,18},{3,19},{4,20},{5,21},{6,22},{7,23},{8,24},{9,... | collective-permute-start | bytes 442376 | tf_op jit(solution)/shard_map/ppermute | solution.py:85
  594.9 18.1 %collective-permute-start.71 = (bf16[192,384]{1,0:T(8,128)(2,1)S(1)}, bf16[192,384]{1,0:T(8,128)(2,1)S(1)}, u32[]{:S(2)}, u32[]{:S(2)}) collective-permute-start(bf16[192,384]{1,0:T(8,128)(2,1)S(1)} %get-tuple-element.127), channel_id=1, source_target_pairs={{0,24},{1,25},{2,26},{3,27},{4,28},{5,29},{6,30},{7,31},{8,16},{9,... | collective-permute-start | bytes 442376 | tf_op jit(solution)/shard_map/ppermute | solution.py:85
  600.6 12.6 %collective-permute-start.79 = (bf16[48,1536]{1,0:T(8,128)(2,1)S(1)}, bf16[48,1536]{1,0:T(8,128)(2,1)S(1)}, u32[]{:S(2)}, u32[]{:S(2)}) collective-permute-start(bf16[48,1536]{1,0:T(8,128)(2,1)S(1)} %fusion.88), channel_id=1, source_target_pairs={{0,1},{1,0},{2,3},{3,2},{4,5},{5,4},{6,7},{7,6},{8,9},{9,8},{10,11... | collective-permute-start | bytes 442376 | tf_op jit(solution)/shard_map/ppermute | solution.py:85
  (165 other events, 1042.5 us)
